TPU v7x, 128 devices: a whole 4x4x4 slice. The times are simulated.
128 devices in a mesh: row: 8 (over y_lo, z), col: 16 (over x, y_hi, core).
Axes of the slice: x: 4, y: 4 (y_hi: 2, y_lo: 2; y = y_hi * 2 + y_lo), z: 4, core: 2. Of those that a mesh axis runs over, the one named last changes fastest.
Arguments:
- amplitudes: float32 [512, 20480], P('row', 'col'), may hold values from -6 to 6
- integrals: float32 [512, 38400], P('col', 'row'), may hold values from -0.25 to 0.25
Outputs:
- residual: float32 [38400, 20480], P('row', 'col')
All inputs are finite; a program needn't handle non-finite values.
Results may differ from a plain program's by a relative error of at most 0.00007.
Values sent between devices are 32-bit elements; how exact they have to be, the bound alone decides.
No kernel may reach another device: no remote copies, remote signals or barrier semaphores. Data moves between devices by JAX's collectives and lax.ppermute only.
A program may use at most 128 MiB of HBM per device.

v0:
```python
import jax
import jax.numpy as jnp
from jax import lax
from jax.sharding import PartitionSpec as P


def contract_rows(left_block, right_block):
    return lax.dot_general(
        left_block,
        right_block,
        (((0,), (0,)), ((), ())),
        precision=lax.Precision.HIGHEST,
        preferred_element_type=jnp.float32,
    )


def ladder(amps_block, integral_block):
    whole_amps = lax.all_gather(amps_block, "row", axis=0, tiled=True)
    return contract_rows(lax.all_gather(integral_block, "col", axis=0, tiled=True), whole_amps)


def body(amplitudes, integrals):
    return 0.5 * ladder(amplitudes, integrals)


def solution(mesh):
    in_specs = (P("row", "col"), P("col", "row"))
    out_specs = P("row", "col")
    return jax.shard_map(body, mesh=mesh, in_specs=in_specs, out_specs=out_specs, check_vma=False)
```

profile of v0, /device:TPU:1, one launch (start us, length us, event | category | flops | bytes accessed | tf_op | source)
XLA Modules:
  0.0 227.3 jit_solution(12496698475896982546)
XLA Ops:
  6.5 0.0 all-gather.5.cloned.1.call-start
  6.5 0.7 all-gather.5.cloned.1.call-update
  7.3 0.0 all-gather.3.cloned.1.call-start
  7.3 0.7 all-gather.3.cloned.1.call-update
  8.0 42.6 %all-gather.5.cloned.1.call-done = f32[512,1280]{1,0:T(8,128)} async-done(((f32[64,1280]{1,0:T(8,128)}), f32[512,1280]{1,0:T(8,128)}) %all-gather.5.cloned.1.call-update) | async-done | bytes 2621456 | tf_op jit(solution)/shard_map/all_gather | solution.py:18
  50.6 85.5 %all-gather.3.cloned.1.call-done = f32[512,4800]{1,0:T(8,128)} async-done(((f32[32,4800]{1,0:T(8,128)}), f32[512,4800]{1,0:T(8,128)}) %all-gather.3.cloned.1.call-update) | async-done | bytes 9830416 | tf_op jit(solution)/shard_map/all_gather | solution.py:19
  136.0 84.5 %convolution_multiply_fusion = f32[4800,1280]{1,0:T(8,128)} fusion(f32[512,4800]{1,0:T(8,128)} %all-gather.3.cloned.1.call-done, f32[512,1280]{1,0:T(8,128)} %all-gather.5.cloned.1.call-done), kind=kOutput, calls=%fused_computation | convolution fusion | flops 37754880000 | bytes 37027840 | tf_op jit(solution)/shard_map/dot_general | solution.py:8
Async XLA Ops:
  6.5 44.0 %all-gather.5.cloned.1.call-start = ((), (), s32[]{:S(2)}) async-start(), calls=%async_computation.1 | async-start | bytes 2949120 | tf_op jit(solution)/shard_map/all_gather | solution.py:18
  7.3 128.8 %all-gather.3.cloned.1.call-start = ((), (), s32[]{:S(2)}) async-start(), calls=%async_computation | async-start | bytes 10584064 | tf_op jit(solution)/shard_map/all_gather | solution.py:19
Sparse Core Ops, SparseCore 0:
  9.0 41.5 all-gather.4
  53.0 83.0 all-gather.2
where the time goes:
time: 227 us
  waiting for transfers between devices  129 us (57%)
  matrix products  84.5 us (37%)
  between operations  13.4 us (6%)
    all_gather x1, waiting for transfers between devices, ladder(): lax.all_gather(integral_block, 'col', axis=0, tiled=True)  85.5 us
    dot_general x1, matrix products, contract_rows(): lax.dot_general(left_block, right_block, (((0,), (0,)), ((), ())), precis...  84.5 us
    all_gather x1, waiting for transfers between devices, ladder(): whole_amps = lax.all_gather(amps_block, 'row', axis=0, tiled=True)  42.6 us
  transfers between devices with their start and end apart: 2, of which 2 were waited for; matrix products, arithmetic and copies ran while one was open for 0% of the time, Pallas kernels for 0%

commit v1 on v0

--- a/solution.py
+++ b/solution.py
@@ -15,7 +15,8 @@
 
 
 def ladder(amps_block, integral_block):
-    whole_amps = lax.all_gather(amps_block, "row", axis=0, tiled=True)
+    sent = jnp.stack([amps_block] * lax.axis_size("row"))
+    whole_amps = jnp.concatenate(lax.all_to_all(sent, "row", 0, 0), axis=0)
     return contract_rows(lax.all_gather(integral_block, "col", axis=0, tiled=True), whole_amps)
 
 

time: 227 us -> 152 us (0.67)
  waiting for transfers between devices: 129 us -> 47.1 us
  blocking collectives: 0 us -> 44.4 us
  matrix products: 84.5 us -> 45.9 us
    all_to_all x0 -> x1, blocking collectives: none -> 44.4 us  [ladder(): whole_amps = jnp.concatenate(lax.all_to_all(sent, 'row', 0, 0), axis=0)]
    all_gather x1 -> x0, waiting for transfers between devices: 42.6 us -> none  [ladder(): whole_amps = lax.all_gather(amps_block, 'row', axis=0, tiled=True)]
    all_gather x1, waiting for transfers between devices: 85.5 us -> 46.4 us  [ladder(): lax.all_gather(integral_block, 'col', axis=0, tiled=True)]
    dot_general x1, matrix products: 84.5 us -> 45.9 us  [contract_rows(): lax.dot_general(left_block, right_block, (((0,), (0,)), ((), ())), precis...]
  transfers between devices with their start and end apart: 2 -> 1, of which waited for: 2 -> 1; matrix products, arithmetic and copies ran while one was open for 0% -> 1% of each run, Pallas kernels for 0% -> 0%
where the time goes in v1:
time: 152 us
  waiting for transfers between devices  47.1 us (31%)
  matrix products  45.9 us (30%)
  blocking collectives  44.4 us (29%)
  between operations  13.4 us (9%)
    all_gather x1, waiting for transfers between devices, ladder(): lax.all_gather(integral_block, 'col', axis=0, tiled=True)  46.4 us
    dot_general x1, matrix products, contract_rows(): lax.dot_general(left_block, right_block, (((0,), (0,)), ((), ())), precis...  45.9 us
    all_to_all x1, blocking collectives, ladder(): whole_amps = jnp.concatenate(lax.all_to_all(sent, 'row', 0, 0), axis=0)  44.4 us
  transfers between devices with their start and end apart: 1, of which 1 were waited for; matrix products, arithmetic and copies ran while one was open for 1% of the time, Pallas kernels for 0%

profile of v1, /device:TPU:1, one launch (start us, length us, event | category | flops | bytes accessed | tf_op | source)
XLA Modules:
  0.0 152.0 jit_solution(2585463985937343268)
XLA Ops:
  6.5 0.0 all-gather.2.cloned.1.call-start
  6.5 0.7 all-gather.2.cloned.1.call-update
  7.3 1.2 stack.2
  8.4 44.4 %all_to_all.5 = f32[8,64,1280]{2,1,0:T(8,128)S(1)} all-to-all(f32[8,64,1280]{2,1,0:T(8,128)S(1)} %stack.2), channel_id=1, replica_groups=mesh['row'=8,'col'=16] {'row'}, dimensions={0} | all-to-all | bytes 5242880 | tf_op jit(solution)/shard_map/all_to_all | solution.py:19
  52.9 46.4 %all-gather.2.cloned.1.call-done = f32[512,4800]{1,0:T(8,128)} async-done(((f32[32,4800]{1,0:T(8,128)}), f32[512,4800]{1,0:T(8,128)}) %all-gather.2.cloned.1.call-update) | async-done | bytes 9830416 | tf_op jit(solution)/shard_map/all_gather | solution.py:20
  99.2 45.9 %convolution_multiply_fusion = f32[4800,1280]{1,0:T(8,128)} fusion(f32[512,4800]{1,0:T(8,128)} %all-gather.2.cloned.1.call-done, f32[512,1280]{1,0:T(8,128)S(1)} %bitcast.3), kind=kOutput, calls=%fused_computation | convolution fusion | flops 37754880000 | bytes 37027840 | tf_op jit(solution)/shard_map/dot_general | solution.py:8
Async XLA Ops:
  6.5 92.7 %all-gather.2.cloned.1.call-start = ((), (), s32[]{:S(2)}) async-start(), calls=%async_computation.1 | async-start | bytes 10584064 | tf_op jit(solution)/shard_map/all_gather | solution.py:20
Sparse Core Ops, SparseCore 0:
  9.8 89.4 all-gather.1
